TPU v7x, 512 devices: a whole 4x8x8 slice. The times are simulated.
512 devices in a mesh: inst: 32 (over x, z), head: 16 (over y, core).
Axes of the slice: x: 4, y: 8, z: 8, core: 2. Of those that a mesh axis runs over, the one named last changes fastest.
Arguments:
- hidden_rows: bfloat16 [32, 32, 16, 9216], P('inst', None, None, 'head'), may hold values from -6 to 6
- send_counts: int32 [32, 32], P('inst'), may hold values from 0 to 16, as said below
- row_session: int32 [32, 32, 16], P('inst'), may hold values from 0 to 1, as said below
- row_position: int32 [32, 32, 16], P('inst'), may hold values from 0 to 1023, as said below
- resident_lengths: int32 [64], P('inst'), may hold values from 1 to 512, as said below
- kv_weight: bfloat16 [9216, 12288], P('inst', 'head'), may hold values from -0.0625 to 0.0625
- key_cache: bfloat16 [64, 1024, 6144], P('inst', None, 'head'), as said below
- value_cache: bfloat16 [64, 1024, 6144], P('inst', None, 'head'), may hold values from -6 to 6
- query: bfloat16 [64, 6144], P('inst', 'head'), as said below
- new_key: bfloat16 [64, 6144], P('inst', 'head'), may hold values from -6 to 6
- new_value: bfloat16 [64, 6144], P('inst', 'head'), may hold values from -6 to 6
Outputs:
- attended: bfloat16 [64, 6144], P('inst', 'head')
Inputs may be any that keep to these rules, and one draw needn't show every extreme that they name: `send_counts`: at most 16 live slots from one source to one destination; in every draw one destination instance receives 16 rows from every source. `row_session`: for a live slot, a session of the destination instance; 0 in slots that are not live. The destination that receives 16 rows from every source sends all of them to one of its sessions. `row_position`: the live rows of one destination session take each of the positions from its resident length to its resident length plus their number minus 1 exactly once; 0 in slots that are not live. In every draw some session's rows end at position 1023. `resident_lengths`: A session's resident length plus its restored rows stays within 1024 positions. `key_cache`: entries of order one. `query`: entries of order one or a few tens.
All inputs are finite; a program needn't handle non-finite values.
Results may differ from a plain program's by a relative error of at most 0.009.
Values may be sent and summed in bfloat16 or wider, within the bound.
No kernel may reach another device: no remote copies, remote signals or barrier semaphores. Data moves between devices by JAX's collectives and lax.ppermute only.
A program may use at most 192 MiB of HBM per device.

v0:
```python
import math
import jax
import jax.numpy as jnp
from jax import lax
from jax.sharding import PartitionSpec as P

HDIM = 128
masked_score = -1e30


def local(
    hidden_rows,
    send_counts,
    row_session,
    row_position,
    resident_lengths,
    kv_weight,
    key_cache,
    value_cache,
    query,
    new_key,
    new_value,
):
    sources = hidden_rows.shape[1]
    slot_cap = hidden_rows.shape[2]
    slot_count = sources * slot_cap
    head_dev = query.shape[1] // HDIM
    sessions_dev = key_cache.shape[0]
    context = key_cache.shape[1]
    inverse_root = 1.0 / math.sqrt(HDIM)
    arrived, counts_in, session_in, position_in = (
        lax.all_to_all(hidden_rows, "inst", split_axis=1, concat_axis=0, tiled=True),
        lax.all_to_all(send_counts, "inst", split_axis=1, concat_axis=0, tiled=True),
        lax.all_to_all(row_session, "inst", split_axis=1, concat_axis=0, tiled=True),
        lax.all_to_all(row_position, "inst", split_axis=1, concat_axis=0, tiled=True),
    )
    full_rows = lax.all_gather(
        arrived.reshape(slot_count, arrived.shape[3]), "head", axis=1, tiled=True
    )
    restored = jnp.dot(
        full_rows,
        lax.all_gather(kv_weight, "inst", axis=0, tiled=True),
        preferred_element_type=jnp.float32,
    )
    restored = restored.astype(jnp.bfloat16).reshape(slot_count, head_dev, 2, HDIM)
    restored_keys = restored[:, :, 0]
    restored_values = restored[:, :, 1]
    slot_live = (jnp.arange(slot_cap)[None, :] < counts_in).reshape(slot_count)
    session_map = session_in.reshape(slot_count)
    position_map = position_in.reshape(slot_count)
    member = (session_map[None, :] == jnp.arange(sessions_dev)[:, None]) & slot_live[None, :]
    queries = query.reshape(sessions_dev, head_dev, HDIM)
    cache_keys = key_cache.reshape(sessions_dev, context, head_dev, HDIM)
    cache_values = value_cache.reshape(sessions_dev, context, head_dev, HDIM)
    own_score = (
        jnp.sum(
            queries.astype(jnp.float32)
            * new_key.reshape(sessions_dev, head_dev, HDIM).astype(jnp.float32),
            axis=-1,
        )
        * inverse_root
    )
    fresh_value = new_value.reshape(sessions_dev, head_dev, HDIM).astype(jnp.float32)
    position_ids = jnp.arange(context)
    target = jnp.where(slot_live, position_map, context)
    key_rows = cache_keys.at[session_map, target].set(restored_keys, mode="drop")
    value_rows = cache_values.at[session_map, target].set(restored_values, mode="drop")
    totals = resident_lengths + jnp.sum(member.astype(jnp.int32), axis=1)
    scores = (
        jnp.einsum("shd,sphd->shp", queries, key_rows, preferred_element_type=jnp.float32)
        * inverse_root
    )
    scores = jnp.where((position_ids[None, :] < totals[:, None])[:, None, :], scores, masked_score)
    highest = jnp.maximum(jnp.max(scores, axis=-1), own_score)
    weights = jnp.exp(scores - highest[:, :, None])
    own_weight = jnp.exp(own_score - highest)
    denominator = jnp.sum(weights, axis=-1) + own_weight
    probability = (weights / denominator[:, :, None]).astype(jnp.bfloat16)
    attended = jnp.einsum(
        "shp,sphd->shd", probability, value_rows, preferred_element_type=jnp.float32
    )
    own_prob = (own_weight / denominator).astype(jnp.bfloat16)
    attended = attended + own_prob.astype(jnp.float32)[:, :, None] * fresh_value
    return attended.astype(jnp.bfloat16).reshape(sessions_dev, head_dev * HDIM)


def solution(mesh):
    placed = (
        P("inst", None, None, "head"),
        P("inst", None),
        P("inst", None, None),
        P("inst", None, None),
        P("inst"),
        P("inst", "head"),
        P("inst", None, "head"),
        P("inst", None, "head"),
        P("inst", "head"),
        P("inst", "head"),
        P("inst", "head"),
    )
    return jax.shard_map(
        local, mesh=mesh, in_specs=placed, out_specs=P("inst", "head"), check_vma=False
    )
```

profile of v0, /device:TPU:1, one launch (start us, length us, event | category | flops | bytes accessed | tf_op | source)
XLA Modules:
  0.0 339.8 jit_solution(13822352009684851430)
XLA Ops:
  6.5 0.0 copy-start.4
  6.6 0.0 copy-start.1
  6.6 0.0 all-gather.3.cloned.1.call-start
  6.6 30.2 %all_to_all.40 = bf16[1,32,16,576]{3,2,0,1:T(8,128)(2,1)S(1)} all-to-all(bf16[1,32,16,576]{3,2,0,1:T(8,128)(2,1)} %bitcast.46), channel_id=1, replica_groups=mesh['inst'=32,'head'=16] {'inst'}, dimensions={1} | all-to-all | bytes 1179648 | tf_op jit(solution)/shard_map/all_to_all | solution.py:32
  36.9 1.1 copy.77
  37.9 0.0 all-gather.3.cloned.1.call-update
  37.9 0.0 all-gather.5.cloned.1.call-start
  38.0 0.7 all-gather.5.cloned.1.call-update
  38.7 0.0 copy-done.8
  38.7 0.7 copy.73
  39.4 8.4 %all-to-all-start.1 = ((s32[1,32,1]{2,0,1:T(1,128)}), s32[1,32,1]{2,0,1:T(1,128)S(1)}, u32[]{:S(2)}, u32[]{:S(2)}) async-start(s32[1,32,1]{2,0,1:T(1,128)} %copy.73), calls=%async_computation.1 | async-start | bytes 32768 | tf_op jit(solution)/shard_map/all_to_all | solution.py:33
  47.8 0.0 copy-done.5
  47.8 0.0 copy-done.6
  47.8 0.0 copy-done.3
  47.9 0.7 copy.72
  48.5 7.9 %all-to-all-done.1 = s32[1,32,1]{2,0,1:T(1,128)S(1)} async-done(((s32[1,32,1]{2,0,1:T(1,128)}), s32[1,32,1]{2,0,1:T(1,128)S(1)}, u32[]{:S(2)}, u32[]{:S(2)}) %all-to-all-start.1) | async-done | bytes 160 | tf_op jit(solution)/shard_map/all_to_all | solution.py:33
  56.4 3.8 %all-to-all-start = ((s32[1,32,16]{2,0,1:T(1,128)}), s32[1,32,16]{2,0,1:T(1,128)S(1)}, u32[]{:S(2)}, u32[]{:S(2)}) async-start(s32[1,32,16]{2,0,1:T(1,128)} %copy.72), calls=%async_computation | async-start | bytes 32768 | tf_op jit(solution)/shard_map/all_to_all | solution.py:34
  60.2 0.1 multiply_reduce_fusion
  60.3 0.1 copy.81
  60.4 0.0 copy-done.7
  60.4 0.0 copy-done.4
  60.4 0.7 copy.75
  61.1 0.0 copy-done.1
  61.1 0.7 copy.74
  61.9 0.0 copy-start.2
  61.9 2.6 copy.79
  64.5 0.0 copy-done.2
  64.5 0.7 copy.82
  65.3 0.0 copy-start.9
  65.3 2.6 copy.84
  67.9 0.7 reduce.1
  68.5 0.3 all-to-all-done
  68.8 9.1 %all-to-all-start.2 = ((s32[1,32,16]{2,0,1:T(1,128)}), s32[1,32,16]{2,0,1:T(1,128)S(1)}, u32[]{:S(2)}, u32[]{:S(2)}) async-start(s32[1,32,16]{2,0,1:T(1,128)} %copy.75), calls=%async_computation.2 | async-start | bytes 32768 | tf_op jit(solution)/shard_map/all_to_all | solution.py:35
  77.9 0.1 iota_compare_fusion
  78.0 0.1 lt.77
  78.1 0.1 lt.81
  78.2 0.1 reshape.176
  78.3 0.5 broadcast.131
  78.8 0.7 reduce.10
  79.5 0.1 eq.15
  79.6 6.8 %all-to-all-done.2 = s32[1,32,16]{2,0,1:T(1,128)S(1)} async-done(((s32[1,32,16]{2,0,1:T(1,128)}), s32[1,32,16]{2,0,1:T(1,128)S(1)}, u32[]{:S(2)}, u32[]{:S(2)}) %all-to-all-start.2) | async-done | bytes 2080 | tf_op jit(solution)/shard_map/all_to_all | solution.py:35
  86.4 0.7 reduce.9
  87.1 0.1 reshape.177
  87.2 0.1 fusion.8
  87.3 0.0 copy-done.9
  87.3 0.1 iota_compare_fusion.1
  87.4 15.0 %all-gather.3.cloned.1.call-done = bf16[512,9216]{0,1:T(8,128)(2,1)} async-done(((bf16[512,576]{0,1:T(8,128)(2,1)}), bf16[512,9216]{0,1:T(8,128)(2,1)}) %all-gather.3.cloned.1.call-update) | async-done | bytes 9437200 | tf_op jit(solution)/shard_map/all_gather | solution.py:37
  102.4 135.1 %all-gather.5.cloned.1.call-done = bf16[9216,768]{1,0:T(8,128)(2,1)} async-done(((bf16[288,768]{1,0:T(8,128)(2,1)}), bf16[9216,768]{1,0:T(8,128)(2,1)}) %all-gather.5.cloned.1.call-update) | async-done | bytes 14155792 | tf_op jit(solution)/shard_map/all_gather | solution.py:42
  237.4 14.2 %convolution_convert_fusion = bf16[512,768]{1,0:T(8,128)(2,1)S(1)} fusion(bf16[512,9216]{0,1:T(8,128)(2,1)} %all-gather.3.cloned.1.call-done, bf16[9216,768]{1,0:T(8,128)(2,1)} %all-gather.5.cloned.1.call-done), kind=kOutput, calls=%fused_computation.6 | convolution fusion | flops 7248150528 | bytes 24379392 | tf_op jit(solution)/shard_map/dot_general | solution.py:40
  251.6 0.2 reshape.179
  251.8 1.1 fusion.15
  252.9 0.1 copy_bitcast_fusion
  253.1 0.3 copy.85
  253.4 0.3 copy.80
  253.8 55.4 %scatter_fusion = bf16[2,1024,3,128]{3,2,1,0:T(4,128)(2,1)} fusion(bf16[2,1024,3,128]{3,2,1,0:T(4,128)(2,1)} %copy.79, s32[512]{0:T(512)S(1)} %bitcast.41, bf16[512,3,128]{2,1,0:T(4,128)(2,1)S(1)} %copy.80), kind=kCustom, calls=%fused_computation | custom fusion | bytes 1183744 | tf_op jit(solution)/shard_map/scatter | solution.py:66
  309.2 2.1 fusion.2
  311.3 0.1 fusion.14
  311.4 0.2 fusion.6
  311.6 0.1 fusion.7
  311.7 0.1 copy.86
  311.8 20.1 %scatter_fusion.1 = bf16[2,1024,3,128]{3,2,1,0:T(4,128)(2,1)S(1)} fusion(bf16[2,1024,3,128]{3,2,1,0:T(4,128)(2,1)S(1)} %copy-done, s32[512]{0:T(512)S(1)} %bitcast.42, bf16[512,3,128]{2,1,0:T(4,128)(2,1)S(1)} %copy.85), kind=kCustom, calls=%fused_computation.1 | custom fusion | bytes 1183744 | tf_op jit(solution)/shard_map/scatter | solution.py:67
  331.9 0.4 fusion
  332.3 0.1 fusion.11
  332.3 0.6 copy.115
  (15 shorter events, 0.1 us)
Async XLA Ops:
  6.5 32.2 %copy-start.8 = (s32[1,32]{1,0:T(1,128)S(1)}, s32[1,32]{1,0:T(1,128)}, u32[]{:S(2)}) copy-start(s32[1,32]{1,0:T(1,128)} %param.12) | copy-start | bytes 388
  6.5 41.3 %copy-start.5 = (bf16[2,384]{1,0:T(2,128)(2,1)S(1)}, bf16[2,384]{1,0:T(2,128)(2,1)}, u32[]{:S(2)}) copy-start(bf16[2,384]{1,0:T(2,128)(2,1)} %param.19) | copy-start | bytes 4612
  6.5 41.3 %copy-start.6 = (bf16[2,384]{1,0:T(2,128)(2,1)S(1)}, bf16[2,384]{1,0:T(2,128)(2,1)}, u32[]{:S(2)}) copy-start(bf16[2,384]{1,0:T(2,128)(2,1)} %param.20) | copy-start | bytes 4612
  6.5 41.3 %copy-start.3 = (s32[1,32,16]{1,2,0:T(8,128)S(1)}, s32[1,32,16]{1,2,0:T(8,128)}, u32[]{:S(2)}) copy-start(s32[1,32,16]{1,2,0:T(8,128)} %param.13) | copy-start | bytes 6148
  6.5 53.9 %copy-start.7 = (bf16[2,384]{1,0:T(2,128)(2,1)S(1)}, bf16[2,384]{1,0:T(2,128)(2,1)}, u32[]{:S(2)}) copy-start(bf16[2,384]{1,0:T(2,128)(2,1)} %param.21) | copy-start | bytes 4612
  6.5 53.9 %copy-start.4 = (s32[1,32,16]{1,2,0:T(8,128)S(1)}, s32[1,32,16]{1,2,0:T(8,128)}, u32[]{:S(2)}) copy-start(s32[1,32,16]{1,2,0:T(8,128)} %param.14) | copy-start | bytes 6148
  6.6 54.5 %copy-start.1 = (bf16[2,1024,384]{2,1,0:T(8,128)(2,1)S(1)}, bf16[2,1024,384]{2,1,0:T(8,128)(2,1)}, u32[]{:S(2)}) copy-start(bf16[2,1024,384]{2,1,0:T(8,128)(2,1)} %param.17) | copy-start | bytes 4718596
  6.6 95.8 %all-gather.3.cloned.1.call-start = ((), (), s32[]{:S(2)}) async-start(), calls=%async_computation.4 | async-start | bytes 10027008 | tf_op jit(solution)/shard_map/all_gather | solution.py:37
  37.9 199.5 %all-gather.5.cloned.1.call-start = ((), (), s32[]{:S(2)}) async-start(), calls=%async_computation.5 | async-start | bytes 14598144 | tf_op jit(solution)/shard_map/all_gather | solution.py:42
  39.4 17.0 %all-to-all-start.1 = ((s32[1,32,1]{2,0,1:T(1,128)}), s32[1,32,1]{2,0,1:T(1,128)S(1)}, u32[]{:S(2)}, u32[]{:S(2)}) async-start(s32[1,32,1]{2,0,1:T(1,128)} %copy.73), calls=%async_computation.1 | async-start | bytes 32768 | tf_op jit(solution)/shard_map/all_to_all | solution.py:33
  56.4 12.4 %all-to-all-start = ((s32[1,32,16]{2,0,1:T(1,128)}), s32[1,32,16]{2,0,1:T(1,128)S(1)}, u32[]{:S(2)}, u32[]{:S(2)}) async-start(s32[1,32,16]{2,0,1:T(1,128)} %copy.72), calls=%async_computation | async-start | bytes 32768 | tf_op jit(solution)/shard_map/all_to_all | solution.py:34
  61.9 2.6 copy-start.2
  65.3 22.0 %copy-start.9 = (s32[2]{0:T(128)S(1)}, s32[2]{0:T(128)}, u32[]{:S(2)}) copy-start(s32[2]{0:T(128)} %param.15) | copy-start | bytes 28
  68.8 17.6 %all-to-all-start.2 = ((s32[1,32,16]{2,0,1:T(1,128)}), s32[1,32,16]{2,0,1:T(1,128)S(1)}, u32[]{:S(2)}, u32[]{:S(2)}) async-start(s32[1,32,16]{2,0,1:T(1,128)} %copy.75), calls=%async_computation.2 | async-start | bytes 32768 | tf_op jit(solution)/shard_map/all_to_all | solution.py:35
  253.8 58.1 %copy-start = (bf16[2,1024,3,128]{3,2,1,0:T(4,128)(2,1)S(1)}, bf16[2,1024,3,128]{3,2,1,0:T(4,128)(2,1)}, u32[]{:S(2)}) copy-start(bf16[2,1024,3,128]{3,2,1,0:T(4,128)(2,1)} %copy.84) | copy-start | bytes 4718596
Sparse Core Ops, SparseCore 0:
  38.1 64.2 all-gather.2
  105.5 131.8 all-gather.4
where the time goes:
time: 341 us; the launch traced here: 340 us
  waiting for transfers between devices  166 us (49%)
  local copies, waits for them, and re-layouts  89.2 us (26%)
  blocking collectives  30.2 us (9%)
  starting transfers between devices  21.4 us (6%)
  matrix products  16.6 us (5%)
  between operations  13.6 us (4%)
    all_gather x1, waiting for transfers between devices, local(): lax.all_gather(kv_weight, 'inst', axis=0, tiled=True)  135 us
    scatter x1, local copies, waits for them, and re-layouts, local(): cache_keys.at[session_map, target].set(restored_keys, mode='drop')  55.4 us
    all_to_all x1, blocking collectives, local(): lax.all_to_all(hidden_rows, 'inst', split_axis=1, concat_axis=0, tiled=True)  30.2 us
    scatter x1, local copies, waits for them, and re-layouts, local(): cache_values.at[session_map, target].set(restored_values, mode='drop')  20.1 us
    all_gather x1, waiting for transfers between devices, local(): lax.all_gather(arrived.reshape(slot_count, arrived.shape[3]), 'head', axi...  15 us
    dot_general x1, matrix products, local(): jnp.dot(full_rows, lax.all_gather(kv_weight, 'inst', axis=0, tiled=True),...  14.2 us
    all_to_all x1, starting transfers between devices, local(): lax.all_to_all(row_position, 'inst', split_axis=1, concat_axis=0, tiled=T...  9.1 us
    all_to_all x1, starting transfers between devices, local(): lax.all_to_all(send_counts, 'inst', split_axis=1, concat_axis=0, tiled=True)  8.39 us
  transfers between devices with their start and end apart: 5, of which 5 were waited for; matrix products, arithmetic and copies ran while one was open for 4% of the time, Pallas kernels for 0%

commit v1 on v0

--- a/solution.py
+++ b/solution.py
@@ -37,11 +37,13 @@
     full_rows = lax.all_gather(
         arrived.reshape(slot_count, arrived.shape[3]), "head", axis=1, tiled=True
     )
-    restored = jnp.dot(
-        full_rows,
-        lax.all_gather(kv_weight, "inst", axis=0, tiled=True),
-        preferred_element_type=jnp.float32,
+    _attach_kinds = lambda local_block: jnp.concatenate(
+        lax.all_to_all(
+            jnp.stack([local_block for _ in range(lax.psum(1, "inst"))], 0), "inst", 0, 0
+        ),
+        0,
     )
+    restored = jnp.dot(full_rows, _attach_kinds(kv_weight), preferred_element_type=jnp.float32)
     restored = restored.astype(jnp.bfloat16).reshape(slot_count, head_dev, 2, HDIM)
     restored_keys = restored[:, :, 0]
     restored_values = restored[:, :, 1]

time: 341 us -> 499 us (1.46)
  waiting for transfers between devices: 166 us -> 313 us
    all_to_all x1, waiting for transfers between devices: 0.32 us -> 237 us  [local(): lax.all_to_all(jnp.stack([local_block for _ in range(lax.psum(1, 'inst'))...]
    all_gather x1 -> x0, waiting for transfers between devices: 135 us -> none  [local(): lax.all_gather(kv_weight, 'inst', axis=0, tiled=True)]
    all_gather x1, waiting for transfers between devices: 15 us -> 61.2 us  [local(): lax.all_gather(arrived.reshape(slot_count, arrived.shape[3]), 'head', axi...]
    all_to_all x1, blocking collectives: 30.2 us -> 17.8 us  [local(): lax.all_to_all(hidden_rows, 'inst', split_axis=1, concat_axis=0, tiled=True)]
    all_to_all x0 -> x1, blocking collectives: none -> 11.6 us  [local(): lax.all_to_all(row_session, 'inst', split_axis=1, concat_axis=0, tiled=True)]
    another operation x0 -> x1, local copies, waits for them, and re-layouts: none -> 7.74 us  [local(): jnp.stack([local_block for _ in range(lax.psum(1, 'inst'))], 0)]
    all_to_all x1, starting transfers between devices: 9.1 us -> 3.77 us  [local(): lax.all_to_all(row_position, 'inst', split_axis=1, concat_axis=0, tiled=T...]
    all_to_all x1, starting transfers between devices: 8.39 us -> 13.7 us  [local(): lax.all_to_all(send_counts, 'inst', split_axis=1, concat_axis=0, tiled=True)]
  transfers between devices with their start and end apart: 5 -> 4, of which waited for: 5 -> 4; matrix products, arithmetic and copies ran while one was open for 4% -> 3% of each run, Pallas kernels for 0% -> 0%
where the time goes in v1:
time: 499 us; the launch traced here: 494 us
  waiting for transfers between devices  313 us (63%)
  local copies, waits for them, and re-layouts  93.7 us (19%)
  blocking collectives  29.4 us (6%)
  starting transfers between devices  24.6 us (5%)
  matrix products  16.6 us (3%)
  between operations  13.6 us (3%)
    all_to_all x1, waiting for transfers between devices, local(): lax.all_to_all(jnp.stack([local_block for _ in range(lax.psum(1, 'inst'))...  237 us
    all_gather x1, waiting for transfers between devices, local(): lax.all_gather(arrived.reshape(slot_count, arrived.shape[3]), 'head', axi...  61.2 us
    scatter x1, local copies, waits for them, and re-layouts, local(): cache_keys.at[session_map, target].set(restored_keys, mode='drop')  51.1 us
    scatter x1, local copies, waits for them, and re-layouts, local(): cache_values.at[session_map, target].set(restored_values, mode='drop')  19.8 us
    all_to_all x1, blocking collectives, local(): lax.all_to_all(hidden_rows, 'inst', split_axis=1, concat_axis=0, tiled=True)  17.8 us
    dot_general x1, matrix products, local(): jnp.dot(full_rows, _attach_kinds(kv_weight), preferred_element_type=jnp.f...  14.2 us
    all_to_all x1, starting transfers between devices, local(): lax.all_to_all(send_counts, 'inst', split_axis=1, concat_axis=0, tiled=True)  13.7 us
    all_to_all x1, blocking collectives, local(): lax.all_to_all(row_session, 'inst', split_axis=1, concat_axis=0, tiled=True)  11.6 us
  transfers between devices with their start and end apart: 4, of which 4 were waited for; matrix products, arithmetic and copies ran while one was open for 3% of the time, Pallas kernels for 0%

profile of v1, /device:TPU:1, one launch (start us, length us, event | category | flops | bytes accessed | tf_op | source)
XLA Modules:
  0.0 494.3 jit_solution(8871331640317069051)
XLA Ops:
  6.5 1.3 copy.73
  7.9 13.7 %all-to-all-start.1 = ((s32[1,32,1]{2,0,1:T(1,128)}), s32[1,32,1]{2,0,1:T(1,128)S(1)}, u32[]{:S(2)}, u32[]{:S(2)}) async-start(s32[1,32,1]{2,0,1:T(1,128)} %copy.73), calls=%async_computation.1 | async-start | bytes 32768 | tf_op jit(solution)/shard_map/all_to_all | solution.py:33
  21.6 1.4 copy.75
  23.0 7.2 %all-to-all-done.1 = s32[1,32,1]{2,0,1:T(1,128)S(1)} async-done(((s32[1,32,1]{2,0,1:T(1,128)}), s32[1,32,1]{2,0,1:T(1,128)S(1)}, u32[]{:S(2)}, u32[]{:S(2)}) %all-to-all-start.1) | async-done | bytes 160 | tf_op jit(solution)/shard_map/all_to_all | solution.py:33
  30.2 3.8 all-to-all-start.2
  34.0 0.8 copy.72
  34.8 7.9 %all-to-all-done.2 = s32[1,32,16]{2,0,1:T(1,128)S(1)} async-done(((s32[1,32,16]{2,0,1:T(1,128)}), s32[1,32,16]{2,0,1:T(1,128)S(1)}, u32[]{:S(2)}, u32[]{:S(2)}) %all-to-all-start.2) | async-done | bytes 2080 | tf_op jit(solution)/shard_map/all_to_all | solution.py:35
  42.6 11.6 %all_to_all.45 = s32[1,32,16]{2,0,1:T(1,128)S(1)} all-to-all(s32[1,32,16]{2,0,1:T(1,128)S(1)} %copy.72), channel_id=1, replica_groups=mesh['inst'=32,'head'=16] {'inst'}, dimensions={1} | all-to-all | bytes 4096 | tf_op jit(solution)/shard_map/all_to_all | solution.py:34
  54.2 17.8 %all_to_all.46 = bf16[1,32,16,576]{3,2,0,1:T(8,128)(2,1)S(1)} all-to-all(bf16[1,32,16,576]{3,2,0,1:T(8,128)(2,1)} %bitcast.45), channel_id=1, replica_groups=mesh['inst'=32,'head'=16] {'inst'}, dimensions={1} | all-to-all | bytes 1179648 | tf_op jit(solution)/shard_map/all_to_all | solution.py:32
  72.1 7.7 %stack.2 = bf16[32,288,768]{2,1,0:T(8,128)(2,1)} broadcast(bf16[288,768]{1,0:T(8,128)(2,1)} %param.16), dimensions={1,2} | broadcast | bytes 14598144 | tf_op jit(solution)/shard_map/stack | solution.py:42
  79.8 0.0 copy-start.3
  79.8 6.9 %all-to-all-start.4 = ((bf16[32,288,768]{2,1,0:T(8,128)(2,1)}), bf16[32,288,768]{2,1,0:T(8,128)(2,1)}, u32[]{:S(2)}, u32[]{:S(2)}) async-start(bf16[32,288,768]{2,1,0:T(8,128)(2,1)} %stack.2), calls=%async_computation.4 | async-start | bytes 28311552 | tf_op jit(solution)/shard_map/all_to_all | solution.py:41
  86.7 0.0 copy-start.1
  86.7 0.2 all-gather.2.cloned.1.call-start
  86.9 1.1 copy.77
  88.0 0.0 all-gather.2.cloned.1.call-update
  88.0 0.0 copy-done.3
  88.1 0.0 copy-done.1
  88.1 0.7 copy.74
  88.9 0.0 copy-start.4
  88.9 0.0 copy-start.2
  88.9 2.6 copy.79
  91.4 0.0 copy-done.4
  91.5 0.1 multiply_reduce_fusion
  91.5 0.1 copy.81
  91.6 0.0 copy-done.2
  91.6 0.8 copy.82
  92.4 0.0 copy-start.5
  92.4 0.0 copy-start.6
  92.4 2.5 copy.84
  95.0 0.0 copy-done.5
  95.0 0.7 reduce.1
  95.6 0.1 iota_compare_fusion
  95.7 0.1 lt.81
  95.8 0.1 lt.77
  95.9 0.5 broadcast.133
  96.4 0.7 reduce.9
  97.1 0.1 reshape.182
  97.2 0.1 reshape.181
  97.3 0.7 reduce.10
  98.0 0.1 eq.15
  98.0 0.1 fusion.8
  98.2 0.0 copy-done.6
  98.2 0.1 iota_compare_fusion.1
  98.3 61.2 %all-gather.2.cloned.1.call-done = bf16[512,9216]{0,1:T(8,128)(2,1)} async-done(((bf16[512,576]{0,1:T(8,128)(2,1)}), bf16[512,9216]{0,1:T(8,128)(2,1)}) %all-gather.2.cloned.1.call-update) | async-done | bytes 9437200 | tf_op jit(solution)/shard_map/all_gather | solution.py:37
  159.5 237.1 %all-to-all-done.4 = bf16[32,288,768]{2,1,0:T(8,128)(2,1)} async-done(((bf16[32,288,768]{2,1,0:T(8,128)(2,1)}), bf16[32,288,768]{2,1,0:T(8,128)(2,1)}, u32[]{:S(2)}, u32[]{:S(2)}) %all-to-all-start.4) | async-done | bytes 14155808 | tf_op jit(solution)/shard_map/all_to_all | solution.py:41
  396.6 14.2 %convolution_convert_fusion = bf16[512,768]{1,0:T(8,128)(2,1)S(1)} fusion(bf16[512,9216]{0,1:T(8,128)(2,1)} %all-gather.2.cloned.1.call-done, bf16[9216,768]{1,0:T(8,128)(2,1)} %bitcast.5), kind=kOutput, calls=%fused_computation.6 | convolution fusion | flops 7248150528 | bytes 24379392 | tf_op jit(solution)/shard_map/dot_general | solution.py:46
  410.8 0.2 reshape.185
  411.0 1.1 fusion.15
  412.1 0.1 copy_bitcast_fusion
  412.2 0.3 copy.80
  412.6 0.0 copy-start
  412.6 51.1 %scatter_fusion = bf16[2,1024,3,128]{3,2,1,0:T(4,128)(2,1)} fusion(bf16[2,1024,3,128]{3,2,1,0:T(4,128)(2,1)} %copy.79, s32[512]{0:T(512)S(1)} %bitcast.40, bf16[512,3,128]{2,1,0:T(4,128)(2,1)S(1)} %copy.80), kind=kCustom, calls=%fused_computation | custom fusion | bytes 1183744 | tf_op jit(solution)/shard_map/scatter | solution.py:68
  463.6 2.1 fusion.2
  465.7 0.1 fusion.14
  465.9 0.2 fusion.6
  466.1 0.1 fusion.7
  466.2 0.3 copy.85
  466.5 0.1 copy.86
  466.6 0.0 copy-done
  466.6 19.8 %scatter_fusion.1 = bf16[2,1024,3,128]{3,2,1,0:T(4,128)(2,1)S(1)} fusion(bf16[2,1024,3,128]{3,2,1,0:T(4,128)(2,1)S(1)} %copy-done, s32[512]{0:T(512)S(1)} %bitcast.41, bf16[512,3,128]{2,1,0:T(4,128)(2,1)S(1)} %copy.85), kind=kCustom, calls=%fused_computation.1 | custom fusion | bytes 1183744 | tf_op jit(solution)/shard_map/scatter | solution.py:69
  486.4 0.4 fusion
  486.8 0.1 fusion.11
  486.9 0.6 copy.115
  (8 shorter events, 0.1 us)
Async XLA Ops:
  7.9 22.3 %all-to-all-start.1 = ((s32[1,32,1]{2,0,1:T(1,128)}), s32[1,32,1]{2,0,1:T(1,128)S(1)}, u32[]{:S(2)}, u32[]{:S(2)}) async-start(s32[1,32,1]{2,0,1:T(1,128)} %copy.73), calls=%async_computation.1 | async-start | bytes 32768 | tf_op jit(solution)/shard_map/all_to_all | solution.py:33
  30.2 12.4 %all-to-all-start.2 = ((s32[1,32,16]{2,0,1:T(1,128)}), s32[1,32,16]{2,0,1:T(1,128)S(1)}, u32[]{:S(2)}, u32[]{:S(2)}) async-start(s32[1,32,16]{2,0,1:T(1,128)} %copy.75), calls=%async_computation.2 | async-start | bytes 32768 | tf_op jit(solution)/shard_map/all_to_all | solution.py:35
  79.8 8.2 %copy-start.3 = (bf16[2,384]{1,0:T(2,128)(2,1)S(1)}, bf16[2,384]{1,0:T(2,128)(2,1)}, u32[]{:S(2)}) copy-start(bf16[2,384]{1,0:T(2,128)(2,1)} %param.19) | copy-start | bytes 4612
  79.8 316.8 %all-to-all-start.4 = ((bf16[32,288,768]{2,1,0:T(8,128)(2,1)}), bf16[32,288,768]{2,1,0:T(8,128)(2,1)}, u32[]{:S(2)}, u32[]{:S(2)}) async-start(bf16[32,288,768]{2,1,0:T(8,128)(2,1)} %stack.2), calls=%async_computation.4 | async-start | bytes 28311552 | tf_op jit(solution)/shard_map/all_to_all | solution.py:41
  86.7 1.4 copy-start.1
  86.7 72.8 %all-gather.2.cloned.1.call-start = ((), (), s32[]{:S(2)}) async-start(), calls=%async_computation.5 | async-start | bytes 10027008 | tf_op jit(solution)/shard_map/all_gather | solution.py:37
  88.9 2.6 copy-start.4
  88.9 2.8 copy-start.2
  92.4 2.5 copy-start.5
  92.4 5.8 %copy-start.6 = (s32[2]{0:T(128)S(1)}, s32[2]{0:T(128)}, u32[]{:S(2)}) copy-start(s32[2]{0:T(128)} %param.15) | copy-start | bytes 28
  412.6 54.1 %copy-start = (bf16[2,1024,3,128]{3,2,1,0:T(4,128)(2,1)S(1)}, bf16[2,1024,3,128]{3,2,1,0:T(4,128)(2,1)}, u32[]{:S(2)}) copy-start(bf16[2,1024,3,128]{3,2,1,0:T(4,128)(2,1)} %copy.84) | copy-start | bytes 4718596
Sparse Core Ops, SparseCore 0:
  89.7 69.7 all-gather.1
